TPU v7x, 512 devices: a whole 4x4x16 slice. The times are simulated.
512 devices in a mesh: segment: 4 (over y_lo, core), ctx: 32 (over z, y_hi), head: 4 (over x).
Axes of the slice: x: 4, y: 4 (y_hi: 2, y_lo: 2; y = y_hi * 2 + y_lo), z: 16, core: 2. Of those that a mesh axis runs over, the one named last changes fastest.
Arguments:
- hidden: bfloat16 [4, 8192, 2880], P('segment', 'ctx', 'head'), may hold values from -450 to 450
- merge_weight: bfloat16 [3, 2880, 2880], P(None, 'head', 'segment'), may hold values from -0.0625 to 0.0625
- query_weight: bfloat16 [5760, 2048], P('ctx', ('segment', 'head')), may hold values from -1 to 1
- key_weight: bfloat16 [5760, 256], P('ctx', 'segment'), may hold values from -8 to 8
- value_weight: bfloat16 [5760, 256], P('ctx', 'segment'), may hold values from -0.078125 to 0.078125
- block_order: int32 [64], replicated, may hold values from 0 to 63, each once
Outputs:
- attended: bfloat16 [8192, 2048], P('ctx', ('segment', 'head'))
Inputs may be any that keep to these rules, and one draw needn't show every extreme that they name: `block_order`: a permutation of the sequence blocks.
All inputs are finite; a program needn't handle non-finite values.
Results may differ from a plain program's by a relative error of at most 0.023.
The roundings to bfloat16 on the way count: a program that leaves them out, or rounds other values in their place, can miss the bound.
Values may be sent and summed in bfloat16 or wider, within the bound.
No kernel may reach another device: no remote copies, remote signals or barrier semaphores. Data moves between devices by JAX's collectives and lax.ppermute only.
A program may use at most 64 MiB of HBM per device.

v0:
```python
import math
import jax
import jax.numpy as jnp
from jax import lax
from jax.sharding import PartitionSpec as P

HD = 64


def normalize(matrix):
    widened = matrix.astype(jnp.float32)
    return widened * lax.rsqrt(jnp.mean(widened * widened, axis=-1, keepdims=True) + 1e-06)


def seq_positions(row_ids, order, block_len):
    block_ids = jnp.arange(order.shape[0], dtype=jnp.int32)
    matches = (row_ids // block_len)[:, None] == block_ids[None, :]
    block_first = jnp.sum(jnp.where(matches, order[None, :], 0), axis=1)
    return block_first * block_len + row_ids % block_len


def attend_block(carry, query_heads, query_pos, key_blk, value_blk, key_pos):
    run_max, run_total, accum = carry
    tok_rows, heads_count, head_size = query_heads.shape
    scores = (
        jnp.einsum("tgd,nd->tgn", query_heads, key_blk, preferred_element_type=jnp.float32) * 0.125
    )
    allowed = key_pos[None, None, :] <= query_pos[:, None, None]
    scores = jnp.where(allowed, scores, -1e30)
    new_max = jnp.maximum(run_max, jnp.max(scores, axis=2))
    rescale = jnp.exp(run_max - new_max)
    unscaled = jnp.where(allowed, jnp.exp(scores - new_max[:, :, None]), 0.0)
    run_total = run_total * rescale + jnp.sum(unscaled, axis=2)
    mixed_rows = jnp.einsum(
        "tgn,nd->tgd", unscaled.astype(jnp.bfloat16), value_blk, preferred_element_type=jnp.float32
    )
    grown = accum.reshape(tok_rows, heads_count, head_size) * rescale[:, :, None] + mixed_rows
    return (new_max, run_total, grown.reshape(tok_rows, heads_count * head_size))


def body(hidden, merge_weight, query_weight, key_weight, value_weight, block_order):
    tok_rows = hidden.shape[1]
    block_len = tok_rows // 2
    segments = lax.axis_size("segment")
    heads_here = lax.axis_size("head")
    segment_id = lax.axis_index("segment")
    head_id = lax.axis_index("head")
    ctx_id = lax.axis_index("ctx")
    sections = lax.all_gather(hidden, "segment", axis=0, tiled=True)
    partial_value = jnp.einsum(
        "ktf,kfc->tc", sections[:3], merge_weight, preferred_element_type=jnp.float32
    )
    col_piece = partial_value.shape[1] // heads_here
    summed = lax.psum(partial_value, "head")
    merged_part = lax.dynamic_slice_in_dim(summed, head_id * col_piece, col_piece, 1)
    merged_part = merged_part.astype(jnp.bfloat16)
    embed_part = lax.dynamic_slice_in_dim(sections[3], segment_id * col_piece, col_piece, 1)
    merged_all, embed_mixed = (
        lax.all_gather(merged_part, ("segment", "head"), axis=1, tiled=True),
        lax.all_gather(embed_part, ("segment", "head"), axis=1, tiled=True),
    )
    embed_all = embed_mixed.reshape(tok_rows, segments, heads_here, col_piece).transpose(0, 2, 1, 3)
    embed_all = embed_all.reshape(tok_rows, segments * heads_here * col_piece)
    draft_input = jnp.concatenate([normalize(embed_all), normalize(merged_all)], axis=1).astype(
        jnp.bfloat16
    )
    query_piece = lax.all_gather(query_weight, "ctx", axis=0, tiled=True)
    key_piece = lax.all_gather(key_weight, "ctx", axis=0, tiled=True)
    value_piece = lax.all_gather(value_weight, "ctx", axis=0, tiled=True)
    query_acc = jnp.dot(draft_input, query_piece, preferred_element_type=jnp.float32)
    key_acc = jnp.dot(draft_input, key_piece, preferred_element_type=jnp.float32)
    value_acc = jnp.dot(draft_input, value_piece, preferred_element_type=jnp.float32)
    query_acc, key_acc, value_acc = (query_acc, key_acc, value_acc)
    query_heads = query_acc.astype(jnp.bfloat16).reshape(tok_rows, -1, HD)
    key_vectors = key_acc.astype(jnp.bfloat16)
    value_vectors = value_acc.astype(jnp.bfloat16)
    heads_count = query_heads.shape[1]
    query_pos = seq_positions(
        ctx_id * tok_rows + jnp.arange(tok_rows, dtype=jnp.int32), block_order, block_len
    )
    initial_attn = (
        jnp.full((tok_rows, heads_count), -1e30, jnp.float32),
        jnp.zeros((tok_rows, heads_count), jnp.float32),
        jnp.zeros((tok_rows, heads_count * HD), jnp.float32),
    )
    key_piece = lax.all_gather(key_vectors, "ctx", axis=0, tiled=True)
    value_piece = lax.all_gather(value_vectors, "ctx", axis=0, tiled=True)
    row_count = key_piece.shape[0]
    key_step = math.gcd(row_count, 512)

    def one_block(turn_index, carried):
        offset = turn_index * key_step
        key_blk = lax.dynamic_slice_in_dim(key_piece, offset, key_step, 0)
        value_blk = lax.dynamic_slice_in_dim(value_piece, offset, key_step, 0)
        key_pos = seq_positions(
            offset + jnp.arange(key_step, dtype=jnp.int32), block_order, block_len
        )
        return attend_block(carried, query_heads, query_pos, key_blk, value_blk, key_pos)

    run_max, run_total, accum = lax.fori_loop(0, row_count // key_step, one_block, initial_attn)
    output = accum.reshape(tok_rows, heads_count, HD) / run_total[:, :, None]
    return output.reshape(tok_rows, heads_count * HD).astype(jnp.bfloat16)


def solution(mesh):
    return jax.shard_map(
        body,
        mesh=mesh,
        in_specs=(
            P("segment", "ctx", "head"),
            P(None, "head", "segment"),
            P("ctx", ("segment", "head")),
            P("ctx", "segment"),
            P("ctx", "segment"),
            P(),
        ),
        out_specs=P("ctx", ("segment", "head")),
        check_vma=False,
    )
```

profile of v0, /device:TPU:4, one launch (start us, length us, event | category | flops | bytes accessed | tf_op | source)
XLA Modules:
  0.0 691.7 jit_solution(7909298819602587909)
XLA Ops:
  7.3 38.2 %all-gather.12.cloned.1.call-done = bf16[4,256,720]{1,2,0:T(8,128)(2,1)} async-done(((bf16[1,256,720]{1,2,0:T(8,128)(2,1)}), bf16[4,256,720]{1,2,0:T(8,128)(2,1)}) %all-gather.12.cloned.1.call-update) | async-done | bytes 1474576 | tf_op jit(solution)/shard_map/all_gather | solution.py:49
  47.5 3.6 convolution_bitcast_fusion
  51.1 25.7 %all-reduce.1 = bf16[256,720]{0,1:T(8,128)(2,1)} all-reduce(f32[256,720]{0,1:T(8,128)} %convolution_bitcast_fusion), channel_id=1, replica_groups=mesh['segment'=4,'ctx'=32,'head'=4] {'head'}, use_global_device_ids=true, to_apply=%region_1.0 | all-reduce | flops 184320 | bytes 1105920 | tf_op jit(solution)/shard_map/psum | solution.py:54
  79.0 83.5 %all-gather.4 = bf16[32,180,64]{1,2,0:T(8,128)(2,1)S(1)} all-gather(bf16[1,180,64]{1,2,0:T(8,128)(2,1)S(1)} %bitcast.59), channel_id=1, replica_groups=mesh['segment'=4,'ctx'=32,'head'=4] {'ctx'}, dimensions={0}, use_global_device_ids=true | all-gather | bytes 760320 | tf_op jit(solution)/shard_map/all_gather | solution.py:69
  164.1 3.1 reshape.158
  167.2 31.9 %multiply_reduce_fusion.1 = (f32[256]{0:T(256)S(1)}, f32[256,2880]{0,1:T(8,128)}) fusion(bf16[1,256,2880]{1,0,2:T(2,128)(2,1)} %all-gather.18.cloned.1.call-done), kind=kLoop, calls=%fused_computation.39 | loop fusion | flops 2211584 | bytes 4424704 | tf_op jit(solution)/shard_map/reduce_sum | solution.py:12
  199.1 4.0 reshape.145
  203.2 3.8 copy.26
  207.0 4.1 reshape.144
  211.1 3.4 reshape.159
  214.5 2.4 multiply_reduce_fusion
  222.4 78.1 %all-gather.2 = bf16[32,180,64]{1,2,0:T(8,128)(2,1)S(1)} all-gather(bf16[1,180,64]{1,2,0:T(8,128)(2,1)S(1)} %bitcast.60), channel_id=1, replica_groups=mesh['segment'=4,'ctx'=32,'head'=4] {'ctx'}, dimensions={0}, use_global_device_ids=true | all-gather | bytes 760320 | tf_op jit(solution)/shard_map/all_gather | solution.py:68
  302.0 3.2 reshape.154
  305.2 3.3 convolution_convert_fusion.2
  308.7 9.7 %all-gather.22.cloned.1.call-done = bf16[32,180,128]{2,1,0:T(8,128)(2,1)} async-done(((bf16[1,180,128]{2,1,0:T(8,128)(2,1)}), bf16[32,180,128]{2,1,0:T(8,128)(2,1)}) %all-gather.22.cloned.1.call-update) | async-done | bytes 1474576 | tf_op jit(solution)/shard_map/all_gather | solution.py:67
  318.4 3.3 reshape.156
  321.7 3.0 convolution_convert_fusion
  324.7 127.4 %all-gather.16.cloned.1.call-done = bf16[8192,64]{0,1:T(8,128)(2,1)} async-done(((bf16[256,64]{0,1:T(8,128)(2,1)}), bf16[8192,64]{0,1:T(8,128)(2,1)}) %all-gather.16.cloned.1.call-update) | async-done | bytes 1048592 | tf_op jit(solution)/shard_map/all_gather | solution.py:87
  452.1 132.5 %all-gather.14.cloned.1.call-done = bf16[8192,64]{0,1:T(8,128)(2,1)} async-done(((bf16[256,64]{0,1:T(8,128)(2,1)}), bf16[8192,64]{0,1:T(8,128)(2,1)}) %all-gather.14.cloned.1.call-update) | async-done | bytes 1048592 | tf_op jit(solution)/shard_map/all_gather | solution.py:86
  585.3 98.0 %while.20 = (s32[]{:T(128)}, f32[256,2]{0,1:T(2,128)S(1)}, f32[256,2]{0,1:T(2,128)S(1)}, f32[256,128]{0,1:T(8,128)}, s32[64]{0:T(128)S(1)}, /*index=5*/s32[256]{...) while((s32[]{:T(128)}, f32[256,2]{0,1:T(2,128)S(1)}, ...), condition=%wide.region_8.9_spmd.clone, body=%wide.region_4.8_spmd.clone.sunk | while | flops 69780480 | bytes 4175302 | solution.py:100
  607.6 2.2 convolution_add_fusion.2
  632.1 2.2 convolution_add_fusion.2
  656.5 2.2 convolution_add_fusion.2
  681.0 2.2 convolution_add_fusion.2
  (207 shorter events, 104.7 us)
Async XLA Ops:
  6.5 41.0 %copy-start = (bf16[3,720,720]{2,1,0:T(8,128)(2,1)S(1)}, bf16[3,720,720]{2,1,0:T(8,128)(2,1)}, u32[]{:S(2)}) copy-start(bf16[3,720,720]{2,1,0:T(8,128)(2,1)} %param.9) | copy-start | bytes 9331204
  6.5 39.0 %all-gather.12.cloned.1.call-start = ((), (), s32[]{:S(2)}) async-start(), calls=%async_computation | async-start | bytes 1843200 | tf_op jit(solution)/shard_map/all_gather | solution.py:49
  7.3 160.0 %all-gather.18.cloned.1.call-start = ((), (), s32[]{:S(2)}) async-start(), calls=%async_computation.3 | async-start | bytes 3133440 | tf_op jit(solution)/shard_map/all_gather | solution.py:60
  47.4 163.6 %all-gather.20.cloned.1.call-start = ((), (), s32[]{:S(2)}) async-start(), calls=%async_computation.4 | async-start | bytes 1601536 | tf_op jit(solution)/shard_map/all_gather | solution.py:59
  47.5 31.5 %copy-start.6 = (bf16[180,64]{0,1:T(8,128)(2,1)S(1)}, bf16[180,64]{0,1:T(8,128)(2,1)}, u32[]{:S(2)}) copy-start(bf16[180,64]{0,1:T(8,128)(2,1)} %param.12) | copy-start | bytes 69124
  78.3 240.1 %all-gather.22.cloned.1.call-start = ((), (), s32[]{:S(2)}) async-start(), calls=%async_computation.5 | async-start | bytes 1554432 | tf_op jit(solution)/shard_map/all_gather | solution.py:67
  78.9 373.2 %all-gather.16.cloned.1.call-start = ((), (), s32[]{:S(2)}) async-start(), calls=%async_computation.2 | async-start | bytes 1081344 | tf_op jit(solution)/shard_map/all_gather | solution.py:87
  214.5 2.7 copy-start.1
  216.9 1.9 copy-start.2
  218.8 1.1 copy-start.3
  218.8 2.2 copy-start.5
  219.9 1.1 copy-start.4
  221.0 1.3 copy-start.7
  222.3 362.3 %all-gather.14.cloned.1.call-start = ((), (), s32[]{:S(2)}) async-start(), calls=%async_computation.1 | async-start | bytes 1081344 | tf_op jit(solution)/shard_map/all_gather | solution.py:86
  305.2 3.4 copy-start.8
Sparse Core Ops, SparseCore 0:
  9.5 36.0 all-gather.11
  47.6 58.5 all-gather.17
  108.3 56.1 all-gather.19
  167.5 150.8 all-gather.21
  321.1 130.8 all-gather.15
  454.9 129.7 all-gather.13
where the time goes:
time: 694 us; the launch traced here: 692 us
  waiting for transfers between devices  309 us (45%)
  blocking collectives  187 us (27%)
  matrix products  81 us (12%)
  other arithmetic  63.7 us (9%)
  local copies, waits for them, and re-layouts  36.5 us (5%)
  between operations  13.6 us (2%)
    all_gather x1, waiting for transfers between devices, body(): key_piece = lax.all_gather(key_vectors, 'ctx', axis=0, tiled=True)  133 us
    all_gather x1, waiting for transfers between devices, body(): value_piece = lax.all_gather(value_vectors, 'ctx', axis=0, tiled=True)  127 us
    all_gather x1, blocking collectives, body(): value_piece = lax.all_gather(value_weight, 'ctx', axis=0, tiled=True)  83.5 us
    all_gather x1, blocking collectives, body(): key_piece = lax.all_gather(key_weight, 'ctx', axis=0, tiled=True)  78.1 us
    all_gather x1, waiting for transfers between devices, body(): sections = lax.all_gather(hidden, 'segment', axis=0, tiled=True)  38.2 us
    dot_general x16, matrix products, attend_block(): jnp.einsum('tgn,nd->tgd', unscaled.astype(jnp.bfloat16), value_blk, prefe...  35.4 us
    dot_general x16, matrix products, attend_block(): jnp.einsum('tgd,nd->tgn', query_heads, key_blk, preferred_element_type=jn...  34.5 us
    reduce_sum x2, other arithmetic, normalize(): jnp.mean(widened * widened, axis=-1, keepdims=True) + 1e-06  34.3 us
  transfers between devices with their start and end apart: 6, of which 4 were waited for; matrix products, arithmetic and copies ran while one was open for 11% of the time, Pallas kernels for 0%

commit v1 on v0

--- a/solution.py
+++ b/solution.py
@@ -65,7 +65,15 @@
         jnp.bfloat16
     )
     query_piece = lax.all_gather(query_weight, "ctx", axis=0, tiled=True)
-    key_piece = lax.all_gather(key_weight, "ctx", axis=0, tiled=True)
+    key_piece = jnp.concatenate(
+        lax.all_to_all(
+            jnp.stack(lax.axis_size("ctx") * [key_weight]),
+            axis_name="ctx",
+            split_axis=0,
+            concat_axis=0,
+        ),
+        axis=0,
+    )
     value_piece = lax.all_gather(value_weight, "ctx", axis=0, tiled=True)
     query_acc = jnp.dot(draft_input, query_piece, preferred_element_type=jnp.float32)
     key_acc = jnp.dot(draft_input, key_piece, preferred_element_type=jnp.float32)

time: 694 us -> 720 us (1.037)
  waiting for transfers between devices: 309 us -> 364 us
  blocking collectives: 187 us -> 140 us
  starting transfers between devices: 0.21 us -> 15.3 us
    all_gather x1 -> x0, blocking collectives: 78.1 us -> none  [body(): key_piece = lax.all_gather(key_weight, 'ctx', axis=0, tiled=True)]
    all_gather x1, waiting for transfers between devices: 9.71 us -> 65.8 us  [body(): query_piece = lax.all_gather(query_weight, 'ctx', axis=0, tiled=True)]
    all_gather x1, blocking collectives: 83.5 us -> 115 us  [body(): value_piece = lax.all_gather(value_weight, 'ctx', axis=0, tiled=True)]
    all_to_all x0 -> x1, starting transfers between devices: none -> 14.9 us  [body(): lax.all_to_all(jnp.stack(lax.axis_size('ctx') * [key_weight]), axis_name=...]
    unnamed x22 -> x19, local copies, waits for them, and re-layouts: 14.8 us -> 9.11 us
  transfers between devices with their start and end apart: 6 -> 7, of which waited for: 4 -> 4; matrix products, arithmetic and copies ran while one was open for 11% -> 11% of each run, Pallas kernels for 0% -> 0%
where the time goes in v1:
time: 720 us; the launch traced here: 718 us
  waiting for transfers between devices  364 us (51%)
  blocking collectives  140 us (19%)
  matrix products  80.8 us (11%)
  other arithmetic  66.8 us (9%)
  local copies, waits for them, and re-layouts  36.4 us (5%)
  starting transfers between devices  15.3 us (2%)
  between operations  13.6 us (2%)
    all_gather x1, waiting for transfers between devices, body(): key_piece = lax.all_gather(key_vectors, 'ctx', axis=0, tiled=True)  133 us
    all_gather x1, waiting for transfers between devices, body(): value_piece = lax.all_gather(value_vectors, 'ctx', axis=0, tiled=True)  127 us
    all_gather x1, blocking collectives, body(): value_piece = lax.all_gather(value_weight, 'ctx', axis=0, tiled=True)  115 us
    all_gather x1, waiting for transfers between devices, body(): query_piece = lax.all_gather(query_weight, 'ctx', axis=0, tiled=True)  65.8 us
    all_gather x1, waiting for transfers between devices, body(): sections = lax.all_gather(hidden, 'segment', axis=0, tiled=True)  38.2 us
    dot_general x16, matrix products, attend_block(): jnp.einsum('tgn,nd->tgd', unscaled.astype(jnp.bfloat16), value_blk, prefe...  35.6 us
    reduce_sum x2, other arithmetic, normalize(): jnp.mean(widened * widened, axis=-1, keepdims=True) + 1e-06  34.3 us
    dot_general x16, matrix products, attend_block(): jnp.einsum('tgd,nd->tgn', query_heads, key_blk, preferred_element_type=jn...  34.1 us
  transfers between devices with their start and end apart: 7, of which 4 were waited for; matrix products, arithmetic and copies ran while one was open for 11% of the time, Pallas kernels for 0%

profile of v1, /device:TPU:4, one launch (start us, length us, event | category | flops | bytes accessed | tf_op | source)
XLA Modules:
  0.0 717.8 jit_solution(9066870788544439)
XLA Ops:
  7.3 38.2 %all-gather.11.cloned.1.call-done = bf16[4,256,720]{1,2,0:T(8,128)(2,1)} async-done(((bf16[1,256,720]{1,2,0:T(8,128)(2,1)}), bf16[4,256,720]{1,2,0:T(8,128)(2,1)}) %all-gather.11.cloned.1.call-update) | async-done | bytes 1474576 | tf_op jit(solution)/shard_map/all_gather | solution.py:49
  45.5 3.5 convolution_bitcast_fusion
  49.1 25.1 %all-reduce.1 = bf16[256,720]{0,1:T(8,128)(2,1)} all-reduce(f32[256,720]{0,1:T(8,128)} %convolution_bitcast_fusion), channel_id=1, replica_groups=mesh['segment'=4,'ctx'=32,'head'=4] {'head'}, use_global_device_ids=true, to_apply=%region_1.0 | all-reduce | flops 184320 | bytes 1105920 | tf_op jit(solution)/shard_map/psum | solution.py:54
  78.9 14.9 %all-to-all-start = ((bf16[32,180,64]{1,2,0:T(8,128)(2,1)}), bf16[32,180,64]{1,2,0:T(8,128)(2,1)}, u32[]{:S(2)}, u32[]{:S(2)}) async-start(bf16[32,180,64]{1,2,0:T(8,128)(2,1)} %stack.2), calls=%async_computation | async-start | bytes 2097152 | tf_op jit(solution)/shard_map/all_to_all | solution.py:69
  94.4 115.0 %all-gather.3 = bf16[32,180,64]{1,2,0:T(8,128)(2,1)S(1)} all-gather(bf16[1,180,64]{1,2,0:T(8,128)(2,1)S(1)} %bitcast.58), channel_id=1, replica_groups=mesh['segment'=4,'ctx'=32,'head'=4] {'ctx'}, dimensions={0}, use_global_device_ids=true | all-gather | bytes 760320 | tf_op jit(solution)/shard_map/all_gather | solution.py:77
  211.0 3.1 reshape.162
  214.2 3.4 reshape.163
  217.6 2.2 multiply_reduce_fusion
  219.8 32.1 %multiply_reduce_fusion.1 = (f32[256]{0:T(256)S(1)}, f32[256,2880]{0,1:T(8,128)}) fusion(bf16[1,256,2880]{1,0,2:T(2,128)(2,1)} %all-gather.17.cloned.1.call-done), kind=kLoop, calls=%fused_computation.39 | loop fusion | flops 2211584 | bytes 4424704 | tf_op jit(solution)/shard_map/reduce_sum | solution.py:12
  253.3 4.0 reshape.151
  257.4 3.8 copy.26
  261.2 4.1 reshape.150
  270.2 2.8 copy.28
  273.0 3.2 reshape.148
  276.1 3.3 convolution_convert_fusion.2
  279.6 65.8 %all-gather.21.cloned.1.call-done = bf16[32,180,128]{2,1,0:T(8,128)(2,1)} async-done(((bf16[1,180,128]{2,1,0:T(8,128)(2,1)}), bf16[32,180,128]{2,1,0:T(8,128)(2,1)}) %all-gather.21.cloned.1.call-update) | async-done | bytes 1474576 | tf_op jit(solution)/shard_map/all_gather | solution.py:67
  345.4 3.3 reshape.160
  348.7 3.0 convolution_convert_fusion
  351.7 126.5 %all-gather.15.cloned.1.call-done = bf16[8192,64]{0,1:T(8,128)(2,1)} async-done(((bf16[256,64]{0,1:T(8,128)(2,1)}), bf16[8192,64]{0,1:T(8,128)(2,1)}) %all-gather.15.cloned.1.call-update) | async-done | bytes 1048592 | tf_op jit(solution)/shard_map/all_gather | solution.py:95
  478.3 132.5 %all-gather.13.cloned.1.call-done = bf16[8192,64]{0,1:T(8,128)(2,1)} async-done(((bf16[256,64]{0,1:T(8,128)(2,1)}), bf16[8192,64]{0,1:T(8,128)(2,1)}) %all-gather.13.cloned.1.call-update) | async-done | bytes 1048592 | tf_op jit(solution)/shard_map/all_gather | solution.py:94
  611.5 97.8 %while.20 = (s32[]{:T(128)}, f32[256,2]{0,1:T(2,128)S(1)}, f32[256,2]{0,1:T(2,128)S(1)}, f32[256,128]{0,1:T(8,128)}, s32[64]{0:T(128)S(1)}, /*index=5*/s32[256]{...) while((s32[]{:T(128)}, f32[256,2]{0,1:T(2,128)S(1)}, ...), condition=%wide.region_8.9_spmd.clone, body=%wide.region_4.8_spmd.clone.sunk | while | flops 69780480 | bytes 4175302 | solution.py:108
  615.3 2.2 convolution_add_fusion.2
  621.5 2.2 convolution_add_fusion.2
  627.6 2.2 convolution_add_fusion.2
  (207 shorter events, 107.3 us)
Async XLA Ops:
  6.5 39.0 %copy-start = (bf16[3,720,720]{2,1,0:T(8,128)(2,1)S(1)}, bf16[3,720,720]{2,1,0:T(8,128)(2,1)}, u32[]{:S(2)}) copy-start(bf16[3,720,720]{2,1,0:T(8,128)(2,1)} %param.9) | copy-start | bytes 9331204
  6.5 39.0 %all-gather.11.cloned.1.call-start = ((), (), s32[]{:S(2)}) async-start(), calls=%async_computation.1 | async-start | bytes 1843200 | tf_op jit(solution)/shard_map/all_gather | solution.py:49
  7.3 206.9 %all-gather.19.cloned.1.call-start = ((), (), s32[]{:S(2)}) async-start(), calls=%async_computation.5 | async-start | bytes 1601536 | tf_op jit(solution)/shard_map/all_gather | solution.py:59
  7.3 70.4 %copy-start.5 = (bf16[180,64]{0,1:T(8,128)(2,1)S(1)}, bf16[180,64]{0,1:T(8,128)(2,1)}, u32[]{:S(2)}) copy-start(bf16[180,64]{0,1:T(8,128)(2,1)} %param.11) | copy-start | bytes 69124
  49.1 45.3 %copy-start.6 = (bf16[180,64]{0,1:T(8,128)(2,1)S(1)}, bf16[180,64]{0,1:T(8,128)(2,1)}, u32[]{:S(2)}) copy-start(bf16[180,64]{0,1:T(8,128)(2,1)} %param.12) | copy-start | bytes 69124
  75.8 144.0 %all-gather.17.cloned.1.call-start = ((), (), s32[]{:S(2)}) async-start(), calls=%async_computation.4 | async-start | bytes 3133440 | tf_op jit(solution)/shard_map/all_gather | solution.py:60
  78.9 191.3 %all-to-all-start = ((bf16[32,180,64]{1,2,0:T(8,128)(2,1)}), bf16[32,180,64]{1,2,0:T(8,128)(2,1)}, u32[]{:S(2)}, u32[]{:S(2)}) async-start(bf16[32,180,64]{1,2,0:T(8,128)(2,1)} %stack.2), calls=%async_computation | async-start | bytes 2097152 | tf_op jit(solution)/shard_map/all_to_all | solution.py:69
  93.8 251.6 %all-gather.21.cloned.1.call-start = ((), (), s32[]{:S(2)}) async-start(), calls=%async_computation.6 | async-start | bytes 1554432 | tf_op jit(solution)/shard_map/all_gather | solution.py:67
  94.4 383.9 %all-gather.15.cloned.1.call-start = ((), (), s32[]{:S(2)}) async-start(), calls=%async_computation.3 | async-start | bytes 1081344 | tf_op jit(solution)/shard_map/all_gather | solution.py:95
  219.8 32.1 %copy-start.1 = (f32[2880,256]{1,0:T(8,128)S(1)}, f32[2880,256]{1,0:T(8,128)}, u32[]{:S(2)}) copy-start(f32[2880,256]{1,0:T(8,128)} %reshape.163) | copy-start | bytes 8847364
  265.3 3.4 copy-start.2
  265.3 3.4 copy-start.4
  267.5 1.1 copy-start.3
  269.9 340.9 %all-gather.13.cloned.1.call-start = ((), (), s32[]{:S(2)}) async-start(), calls=%async_computation.2 | async-start | bytes 1081344 | tf_op jit(solution)/shard_map/all_gather | solution.py:94
  276.1 3.4 copy-start.7
Sparse Core Ops, SparseCore 0:
  9.5 36.0 all-gather.10
  75.9 55.6 all-gather.18
  133.7 58.7 all-gather.16
  195.5 149.8 all-gather.20
  348.2 130.0 all-gather.14
  481.0 129.7 all-gather.12
